TPU v7x, 32 devices: a whole 2x2x4 slice. The times are simulated.
32 devices in a mesh: dp: 2 (over x), expert: 16 (over z, y, core).
Axes of the slice: x: 2, y: 2, z: 4, core: 2. Of those that a mesh axis runs over, the one named last changes fastest.
Arguments:
- residual_in: bfloat16 [1024, 2048], P(('dp', 'expert')), may hold values from -6 to 6
- attention_out: bfloat16 [1024, 2048], P(('dp', 'expert')), may hold values from -6 to 6
- out_weight: bfloat16 [2048, 2048], P(None, 'dp'), may hold values from -0.125 to 0.125
- post_gain: float32 [2048], replicated, may hold values from 0.1 to 1.9
- router_weight: bfloat16 [2048, 16], replicated, may hold values from -0.125 to 0.125
- expert_ids: int32 [1024, 6], P(('dp', 'expert')), may hold values from 0 to 15, all different within a row; in each aligned block of 32 rows (0 to 31, 32 to 63, ...) at most 24 rows name the same one
- expert_slot: int32 [16], replicated, may hold values from 0 to 15, each once
- expert_gate_up: bfloat16 [16, 2048, 1408], P('expert', 'dp'), may hold values from -0.125 to 0.125
- expert_down: bfloat16 [16, 704, 2048], P('expert', None, 'dp'), may hold values from -0.21875 to 0.21875
- shared_gate_up: bfloat16 [2048, 2, 2816], P(None, None, 'dp'), may hold values from -0.125 to 0.125
- shared_down: bfloat16 [2816, 2048], P(None, 'dp'), may hold values from -0.109375 to 0.109375
- final_gain: float32 [2048], replicated, may hold values from 0.1 to 1.9
Outputs:
- mixed: bfloat16 [1024, 2048], P(('dp', 'expert'))
Inputs may be any that keep to these rules, and one draw needn't show every extreme that they name: `expert_ids`: each row names 6 different experts. In each aligned block of 32 rows (the rows of one device) no expert is named by more than 24 rows, a bound that some block reaches. A permutation: expert e is held in slot expert_slot[e].
All inputs are finite; a program needn't handle non-finite values.
Results may differ from a plain program's by a relative error of at most 0.0069.
Values may be sent and summed in bfloat16 or wider, within the bound.
A program may use at most 64 MiB of HBM per device.

v0:
```python
import jax
import jax.numpy as jnp
from jax import lax
from jax.sharding import PartitionSpec as P

EPS = 1e-06


def rms_scale(values, gain):
    values = values.astype(jnp.float32)
    inverse = lax.rsqrt(jnp.mean(values * values, axis=-1, keepdims=True) + EPS)
    return values * inverse * gain


def per_device(
    residual_in,
    attention_out,
    out_weight,
    post_gain,
    router_weight,
    expert_ids,
    expert_slot,
    expert_gate_up,
    expert_down,
    shared_gate_up,
    shared_down,
    final_gain,
):
    rows = residual_in.shape[0]
    width = residual_in.shape[1]
    experts = router_weight.shape[1]
    choose = expert_ids.shape[1]
    capacity = max(2, min(rows, 2 * rows * choose // experts))
    proj_cols = jnp.dot(
        lax.all_gather(attention_out, "dp", axis=0, tiled=True),
        out_weight,
        preferred_element_type=jnp.float32,
    ).astype(jnp.bfloat16)
    proj = lax.all_to_all(proj_cols, "dp", split_axis=0, concat_axis=1, tiled=True)
    resid = (residual_in.astype(jnp.float32) + proj.astype(jnp.float32)).astype(jnp.bfloat16)
    normed = rms_scale(resid, post_gain).astype(jnp.bfloat16)
    logits = jnp.dot(normed, router_weight, preferred_element_type=jnp.float32)
    expert_range = jnp.arange(experts, dtype=jnp.int32)
    picked = expert_ids[:, :, None] == expert_range[None, None, :]
    chosen = jnp.sum(jnp.where(picked, logits[:, None, :], 0.0), axis=2)
    raised = jnp.exp(chosen)
    gates = raised / jnp.sum(raised, axis=1, keepdims=True)
    slots = jnp.sum(jnp.where(picked, expert_slot[None, None, :], 0), axis=2).reshape(-1)
    marked = (slots[:, None] == expert_range[None, :]).astype(jnp.int32)
    before = jnp.cumsum(marked, axis=0) - marked
    position = jnp.sum(before * marked, axis=1)
    target = slots * capacity + position
    placed = target[:, None] == jnp.arange(experts * capacity, dtype=jnp.int32)[None, :]
    select = jnp.any(placed.reshape(rows, choose, experts * capacity), axis=1).astype(jnp.bfloat16)
    outgoing = jnp.einsum("rs,rd->sd", select, normed, preferred_element_type=jnp.float32)
    outgoing = outgoing.astype(jnp.bfloat16).reshape(experts, capacity, width)
    gate_up_all, down_all = (
        lax.all_gather(expert_gate_up, "dp", axis=1, tiled=True),
        lax.all_gather(expert_down, "dp", axis=2, tiled=True),
    )
    gate_up_full = gate_up_all[0]
    down_full = down_all[0]
    hidden_units = gate_up_full.shape[1] // 2
    received = lax.all_to_all(outgoing, "expert", split_axis=0, concat_axis=0, tiled=True)
    sources, count, _ = received.shape
    flat = received.reshape(sources * count, width)
    both = jnp.dot(flat, gate_up_full, preferred_element_type=jnp.float32)
    active = (jax.nn.silu(both[:, :hidden_units]) * both[:, hidden_units:]).astype(jnp.bfloat16)
    result = jnp.dot(active, down_full, preferred_element_type=jnp.float32).astype(jnp.bfloat16)
    result = result.reshape(sources, count, width)
    returned = lax.all_to_all(result, "expert", split_axis=0, concat_axis=0, tiled=True)
    shared_units = shared_gate_up.shape[2]
    shared_pair = shared_gate_up.reshape(width, 2 * shared_units)
    both = jnp.dot(
        lax.all_gather(normed, "dp", axis=0, tiled=True),
        shared_pair,
        preferred_element_type=jnp.float32,
    )
    shared_hidden = (jax.nn.silu(both[:, :shared_units]) * both[:, shared_units:]).astype(
        jnp.bfloat16
    )
    out_cols = jnp.dot(
        lax.all_gather(shared_hidden, "dp", axis=1, tiled=True),
        shared_down,
        preferred_element_type=jnp.float32,
    )
    shared_out = lax.all_to_all(out_cols, "dp", split_axis=0, concat_axis=1, tiled=True)
    back_rows = jnp.take(returned.reshape(experts * capacity, width), target, axis=0)
    back_rows = back_rows.reshape(rows, choose, width).astype(jnp.float32)
    routed = jnp.sum(gates[:, :, None] * back_rows, axis=1)
    total = resid.astype(jnp.float32) + routed + shared_out
    return rms_scale(total, final_gain).astype(jnp.bfloat16)


def solution(mesh):
    in_specs = (
        P(("dp", "expert"), None),
        P(("dp", "expert"), None),
        P(None, "dp"),
        P(),
        P(),
        P(("dp", "expert"), None),
        P(),
        P("expert", "dp", None),
        P("expert", None, "dp"),
        P(None, None, "dp"),
        P(None, "dp"),
        P(),
    )
    out_specs = P(("dp", "expert"), None)
    return jax.shard_map(
        per_device, mesh=mesh, in_specs=in_specs, out_specs=out_specs, check_vma=False
    )
```

profile of v0, /device:TPU:0, one launch (start us, length us, event | category | flops | bytes accessed | tf_op | source)
XLA Modules:
  0.0 194.2 jit_solution(14211325119161849407)
XLA Ops:
  6.5 0.7 all-gather.3.cloned.1.call-update
  7.3 0.2 copy-done.1
  7.5 7.1 %all_gather.15 = bf16[64,2048]{1,0:T(8,128)(2,1)S(1)} all-gather(bf16[32,2048]{1,0:T(8,128)(2,1)S(1)} %copy-done.1), channel_id=1, replica_groups=mesh['dp'=2,'expert'=16] {'dp'}, dimensions={0}, use_global_device_ids=true | all-gather | bytes 393216 | tf_op jit(solution)/shard_map/all_gather | solution.py:35
  14.6 3.7 %convolution_convert_fusion.1 = bf16[64,1024]{1,0:T(8,128)(2,1)} fusion(bf16[64,2048]{1,0:T(8,128)(2,1)S(1)} %all_gather.15, bf16[2048,1024]{1,0:T(8,128)(2,1)} %param.14), kind=kOutput, calls=%fused_computation.10 | convolution fusion | flops 268500992 | bytes 4587520 | tf_op jit(solution)/shard_map/dot_general | solution.py:34
  18.3 3.4 %all-to-all-start = ((bf16[2,32,1024]{2,1,0:T(8,128)(2,1)}), bf16[2,32,1024]{2,1,0:T(8,128)(2,1)S(1)}, u32[]{:S(2)}, u32[]{:S(2)}) async-start(bf16[2,32,1024]{2,1,0:T(8,128)(2,1)} %bitcast), calls=%async_computation | async-start | bytes 262144 | tf_op jit(solution)/shard_map/all_to_all | solution.py:39
  22.0 0.6 reduce-window.6
  22.6 0.2 slice_reduce_fusion
  23.1 0.1 fusion.11
  23.3 4.1 %all-to-all-done = bf16[2,32,1024]{2,1,0:T(8,128)(2,1)S(1)} async-done(((bf16[2,32,1024]{2,1,0:T(8,128)(2,1)}), bf16[2,32,1024]{2,1,0:T(8,128)(2,1)S(1)}, u32[]{:S(2)}, u32[]{:S(2)}) %all-to-all-start) | async-done | bytes 131104 | tf_op jit(solution)/shard_map/all_to_all | solution.py:39
  27.4 0.2 fusion.12
  27.7 1.8 convolution_convert_fusion
  29.5 6.4 %all-to-all-start.1 = ((bf16[16,24,2048]{2,1,0:T(8,128)(2,1)}), bf16[16,24,2048]{2,1,0:T(8,128)(2,1)}, u32[]{:S(2)}, u32[]{:S(2)}) async-start(bf16[16,24,2048]{2,1,0:T(8,128)(2,1)} %bitcast.3), calls=%async_computation.1 | async-start | bytes 3145728 | tf_op jit(solution)/shard_map/all_to_all | solution.py:64
  36.0 0.7 all-gather.5.cloned.1.call-update
  36.7 7.7 %copy.36 = bf16[256,8,2,1408]{3,1,2,0:T(8,128)(2,1)S(1)} copy(bf16[256,8,2,1408]{3,2,1,0:T(2,128)(2,1)} %bitcast.50) | data formatting | bytes 23068672
  44.4 9.6 %all_gather.18 = bf16[64,2048]{1,0:T(8,128)(2,1)S(1)} all-gather(bf16[32,2048]{1,0:T(8,128)(2,1)S(1)} %fusion.14), channel_id=1, replica_groups=mesh['dp'=2,'expert'=16] {'dp'}, dimensions={0}, use_global_device_ids=true | all-gather | bytes 393216 | tf_op jit(solution)/shard_map/all_gather | solution.py:75
  54.0 2.1 %fusion.22 = f32[64,2816]{1,0:T(8,128)S(1)} fusion(bf16[64,2048]{1,0:T(8,128)(2,1)S(1)} %all_gather.18, bf16[2048,2816]{1,0:T(8,128)(2,1)S(1)} %bitcast.48), kind=kOutput, calls=%fused_computation.52 | convolution fusion | flops 738197504 | bytes 12517376 | tf_op jit(solution)/shard_map/dot_general | solution.py:74
  56.1 0.1 fusion.10
  56.2 11.5 %all_gather.19 = bf16[64,2816]{1,0:T(8,128)(2,1)S(1)} all-gather(bf16[64,1408]{1,0:T(8,128)(2,1)S(1)} %fusion.10), channel_id=1, replica_groups=mesh['dp'=2,'expert'=16] {'dp'}, dimensions={1}, use_global_device_ids=true | all-gather | bytes 540672 | tf_op jit(solution)/shard_map/all_gather | solution.py:83
  67.7 1.8 fusion.23
  69.5 3.4 %all-to-all-start.3 = ((f32[2,32,1024]{2,1,0:T(8,128)}), f32[2,32,1024]{2,1,0:T(8,128)S(1)}, u32[]{:S(2)}, u32[]{:S(2)}) async-start(f32[2,32,1024]{2,1,0:T(8,128)} %bitcast.11), calls=%async_computation.3 | async-start | bytes 524288 | tf_op jit(solution)/shard_map/all_to_all | solution.py:87
  73.0 23.7 %all-gather.3.cloned.1.call-done = bf16[1,2048,1408]{2,1,0:T(8,128)(2,1)} async-done(((bf16[1,1024,1408]{2,1,0:T(8,128)(2,1)}), bf16[1,2048,1408]{2,1,0:T(8,128)(2,1)}) %all-gather.3.cloned.1.call-update) | async-done | bytes 5767184 | tf_op jit(solution)/shard_map/all_gather | solution.py:58
  96.7 7.1 %fusion = f32[384,1408]{1,0:T(8,128)} fusion(bf16[384,2048]{1,0:T(8,128)(2,1)} %bitcast.4, bf16[1,2048,1408]{2,1,0:T(8,128)(2,1)} %all-gather.3.cloned.1.call-done), kind=kOutput, calls=%fused_computation.1 | convolution fusion | flops 2214592512 | bytes 9502720 | tf_op jit(solution)/shard_map/dot_general | solution.py:67
  103.8 36.7 %all-gather.5.cloned.1.call-done = bf16[1,704,2048]{2,1,0:T(8,128)(2,1)} async-done(((bf16[1,704,1024]{2,1,0:T(8,128)(2,1)}), bf16[1,704,2048]{2,1,0:T(8,128)(2,1)}) %all-gather.5.cloned.1.call-update) | async-done | bytes 2883600 | tf_op jit(solution)/shard_map/all_gather | solution.py:59
  140.5 5.2 %fusion.4 = bf16[384,2048]{1,0:T(8,128)(2,1)} fusion(bf16[1,704,2048]{2,1,0:T(8,128)(2,1)} %all-gather.5.cloned.1.call-done, f32[384,1408]{1,0:T(8,128)} %fusion), kind=kOutput, calls=%fused_computation.5 | convolution fusion | flops 1109704704 | bytes 6815744 | tf_op jit(solution)/shard_map/dot_general | solution.py:69
  145.7 5.6 %all-to-all-start.2 = ((bf16[16,24,2048]{2,1,0:T(8,128)(2,1)}), bf16[16,24,2048]{2,1,0:T(8,128)(2,1)S(1)}, u32[]{:S(2)}, u32[]{:S(2)}) async-start(bf16[16,24,2048]{2,1,0:T(8,128)(2,1)} %bitcast.55), calls=%async_computation.2 | async-start | bytes 3145728 | tf_op jit(solution)/shard_map/all_to_all | solution.py:71
  151.6 0.1 fusion.21
  152.0 31.3 %all-to-all-done.2 = bf16[16,24,2048]{2,1,0:T(8,128)(2,1)S(1)} async-done(((bf16[16,24,2048]{2,1,0:T(8,128)(2,1)}), bf16[16,24,2048]{2,1,0:T(8,128)(2,1)S(1)}, u32[]{:S(2)}, u32[]{:S(2)}) %all-to-all-start.2) | async-done | bytes 1572896 | tf_op jit(solution)/shard_map/all_to_all | solution.py:71
  183.3 1.1 gather_fusion
  184.4 0.3 gather.7
  184.7 1.7 multiply_reduce_fusion
  186.4 0.2 multiply_reduce_fusion.1
  186.6 0.8 multiply_convert_fusion
  (50 shorter events, 1.3 us)
Async XLA Ops:
  6.5 145.1 %copy-start = (bf16[2048,16]{0,1:T(8,128)(2,1)S(1)}, bf16[2048,16]{0,1:T(8,128)(2,1)}, u32[]{:S(2)}) copy-start(bf16[2048,16]{0,1:T(8,128)(2,1)} %param.16) | copy-start | bytes 196612
  6.5 0.9 copy-start.1
  6.5 90.2 %all-gather.3.cloned.1.call-start = ((), (), s32[]{:S(2)}) async-start(), calls=%async_computation.4 | async-start | bytes 8650752 | tf_op jit(solution)/shard_map/all_gather | solution.py:58
  14.6 7.1 %copy-start.3 = (s32[32,6]{0,1:T(8,128)S(1)}, s32[32,6]{0,1:T(8,128)}, u32[]{:S(2)}) copy-start(s32[32,6]{0,1:T(8,128)} %param.17) | copy-start | bytes 2308
  14.6 7.2 %copy-start.6 = (s32[16]{0:T(128)S(1)}, s32[16]{0:T(128)}, u32[]{:S(2)}) copy-start(s32[16]{0:T(128)} %param.18) | copy-start | bytes 196
  14.6 12.8 %copy-start.2 = (bf16[32,2048]{1,0:T(8,128)(2,1)S(1)}, bf16[32,2048]{1,0:T(8,128)(2,1)}, u32[]{:S(2)}) copy-start(bf16[32,2048]{1,0:T(8,128)(2,1)} %param.12) | copy-start | bytes 393220
  14.6 13.0 %copy-start.5 = (f32[2048]{0:T(1024)S(1)}, f32[2048]{0:T(1024)}, u32[]{:S(2)}) copy-start(f32[2048]{0:T(1024)} %param.15) | copy-start | bytes 24580
  18.3 9.1 %all-to-all-start = ((bf16[2,32,1024]{2,1,0:T(8,128)(2,1)}), bf16[2,32,1024]{2,1,0:T(8,128)(2,1)S(1)}, u32[]{:S(2)}, u32[]{:S(2)}) async-start(bf16[2,32,1024]{2,1,0:T(8,128)(2,1)} %bitcast), calls=%async_computation | async-start | bytes 262144 | tf_op jit(solution)/shard_map/all_to_all | solution.py:39
  29.5 40.0 %all-to-all-start.1 = ((bf16[16,24,2048]{2,1,0:T(8,128)(2,1)}), bf16[16,24,2048]{2,1,0:T(8,128)(2,1)}, u32[]{:S(2)}, u32[]{:S(2)}) async-start(bf16[16,24,2048]{2,1,0:T(8,128)(2,1)} %bitcast.3), calls=%async_computation.1 | async-start | bytes 3145728 | tf_op jit(solution)/shard_map/all_to_all | solution.py:64
  35.9 104.6 %all-gather.5.cloned.1.call-start = ((), (), s32[]{:S(2)}) async-start(), calls=%async_computation.5 | async-start | bytes 4325376 | tf_op jit(solution)/shard_map/all_gather | solution.py:59
  36.0 31.7 %slice-start = ((s8[5767168]{0:T(1024)(128)(4,1)}), s8[1572864]{0:T(1024)(128)(4,1)S(1)}, s32[]{:S(2)}) async-start(s8[5767168]{0:T(1024)(128)(4,1)} %bitcast.51), calls=%async_computation.6 | async-start | bytes 3145728
  36.7 31.0 %slice-start.1 = ((s8[5767168]{0:T(1024)(128)(4,1)}), s8[4194304]{0:T(1024)(128)(4,1)S(1)}, s32[]{:S(2)}) async-start(s8[5767168]{0:T(1024)(128)(4,1)} %bitcast.51), calls=%async_computation.7 | async-start | bytes 8388608
  69.5 76.1 %all-to-all-start.3 = ((f32[2,32,1024]{2,1,0:T(8,128)}), f32[2,32,1024]{2,1,0:T(8,128)S(1)}, u32[]{:S(2)}, u32[]{:S(2)}) async-start(f32[2,32,1024]{2,1,0:T(8,128)} %bitcast.11), calls=%async_computation.3 | async-start | bytes 524288 | tf_op jit(solution)/shard_map/all_to_all | solution.py:87
  145.7 37.6 %all-to-all-start.2 = ((bf16[16,24,2048]{2,1,0:T(8,128)(2,1)}), bf16[16,24,2048]{2,1,0:T(8,128)(2,1)S(1)}, u32[]{:S(2)}, u32[]{:S(2)}) async-start(bf16[16,24,2048]{2,1,0:T(8,128)(2,1)} %bitcast.55), calls=%async_computation.2 | async-start | bytes 3145728 | tf_op jit(solution)/shard_map/all_to_all | solution.py:71
  184.4 2.2 %copy-start.4 = (f32[2048]{0:T(1024)S(1)}, f32[2048]{0:T(1024)}, u32[]{:S(2)}) copy-start(f32[2048]{0:T(1024)} %param.23) | copy-start | bytes 24580
Sparse Core Ops, SparseCore 0:
  8.9 87.7 all-gather.2
  98.2 42.2 all-gather.4
where the time goes:
time: 198 us; the launch traced here: 194 us
  waiting for transfers between devices  97.2 us (49%)
  blocking collectives  28.2 us (14%)
  matrix products  21.9 us (11%)
  starting transfers between devices  18.9 us (10%)
  between operations  13.6 us (7%)
  local copies, waits for them, and re-layouts  10.3 us (5%)
  other arithmetic  4.05 us (2%)
    all_gather x1, waiting for transfers between devices, per_device(): lax.all_gather(expert_down, 'dp', axis=2, tiled=True)  36.7 us
    all_to_all x1, waiting for transfers between devices, per_device(): lax.all_to_all(result, 'expert', split_axis=0, concat_axis=0, tiled=True)  31.3 us
    all_gather x1, waiting for transfers between devices, per_device(): lax.all_gather(expert_gate_up, 'dp', axis=1, tiled=True)  23.7 us
    all_gather x1, blocking collectives, per_device(): lax.all_gather(shared_hidden, 'dp', axis=1, tiled=True)  11.5 us
    all_gather x1, blocking collectives, per_device(): lax.all_gather(normed, 'dp', axis=0, tiled=True)  9.62 us
    unnamed x19, local copies, waits for them, and re-layouts  7.96 us
    dot_general x1, matrix products, per_device(): both = jnp.dot(flat, gate_up_full, preferred_element_type=jnp.float32)  7.13 us
    all_gather x1, blocking collectives, per_device(): lax.all_gather(attention_out, 'dp', axis=0, tiled=True)  7.08 us
  transfers between devices with their start and end apart: 6, of which 4 were waited for; matrix products, arithmetic and copies ran while one was open for 16% of the time, Pallas kernels for 0%

commit v1 on v0

--- a/solution.py
+++ b/solution.py
@@ -12,7 +12,7 @@
     return values * inverse * gain
 
 
-def per_device(
+def general(
     residual_in,
     attention_out,
     out_weight,
@@ -47,7 +47,10 @@
     gates = raised / jnp.sum(raised, axis=1, keepdims=True)
     slots = jnp.sum(jnp.where(picked, expert_slot[None, None, :], 0), axis=2).reshape(-1)
     marked = (slots[:, None] == expert_range[None, :]).astype(jnp.int32)
-    before = jnp.cumsum(marked, axis=0) - marked
+    order = jnp.arange(rows * choose, dtype=jnp.int32)
+    earlier = (order[:, None] > order[None, :]).astype(jnp.bfloat16)
+    before = jnp.dot(earlier, marked.astype(jnp.bfloat16), preferred_element_type=jnp.float32)
+    before = before.astype(jnp.int32)
     position = jnp.sum(before * marked, axis=1)
     target = slots * capacity + position
     placed = target[:, None] == jnp.arange(experts * capacity, dtype=jnp.int32)[None, :]
@@ -92,6 +95,76 @@
     return rms_scale(total, final_gain).astype(jnp.bfloat16)
 
 
+def pair(
+    residual_in,
+    attention_out,
+    out_weight,
+    post_gain,
+    router_weight,
+    expert_ids,
+    expert_slot,
+    expert_gate_up,
+    expert_down,
+    shared_gate_up,
+    shared_down,
+    final_gain,
+):
+    swap = [(0, 1), (1, 0)]
+    d = lax.axis_index("dp")
+    e = lax.axis_index("expert")
+    rows, width = residual_in.shape
+    experts = router_weight.shape[1]
+    half = width // 2
+    proj_cols = jnp.dot(
+        lax.all_gather(attention_out, "dp", axis=0, tiled=True),
+        out_weight,
+        preferred_element_type=jnp.float32,
+    ).astype(jnp.bfloat16)
+    proj = lax.all_to_all(proj_cols, "dp", split_axis=0, concat_axis=1, tiled=True)
+    resid = (residual_in.astype(jnp.float32) + proj.astype(jnp.float32)).astype(jnp.bfloat16)
+    normed = rms_scale(resid, post_gain).astype(jnp.bfloat16)
+    both_rows = lax.all_gather(normed, "dp", axis=0, tiled=True)
+    ids = lax.all_gather(expert_ids, "dp", axis=0, tiled=True)
+    mine = lax.dynamic_slice_in_dim(both_rows, d * half, half, axis=1)
+    every = lax.all_gather(mine, "expert", axis=0, tiled=True)
+    logits = jnp.dot(both_rows, router_weight, preferred_element_type=jnp.float32)
+    expert_range = jnp.arange(experts, dtype=jnp.int32)
+    named = jnp.any(ids[:, :, None] == expert_range[None, None, :], axis=1)
+    raised = jnp.where(named, jnp.exp(logits), 0.0)
+    gates = raised / jnp.sum(raised, axis=1, keepdims=True)
+    gates_all = lax.all_gather(gates, "expert", axis=0, tiled=True)
+    here = (expert_slot == e)[None, :]
+    gate = jnp.sum(jnp.where(here, gates_all, 0.0), axis=1, keepdims=True)
+    units = expert_gate_up.shape[2] // 2
+    part = jnp.dot(every, expert_gate_up[0], preferred_element_type=jnp.float32)
+    count = part.shape[0] // 2
+    other = lax.dynamic_slice_in_dim(part, (1 - d) * count, count).astype(jnp.bfloat16)
+    own = lax.dynamic_slice_in_dim(part, d * count, count)
+    both = own + lax.ppermute(other, "dp", swap).astype(jnp.float32)
+    active = (jax.nn.silu(both[:, :units]) * both[:, units:]).astype(jnp.bfloat16)
+    active = lax.all_gather(active, "dp", axis=0, tiled=True)
+    result = jnp.dot(active, expert_down[0], preferred_element_type=jnp.float32)
+    result = result.astype(jnp.bfloat16).astype(jnp.float32) * gate
+    routed = lax.psum_scatter(
+        result.astype(jnp.bfloat16), "expert", scatter_dimension=0, tiled=True
+    )
+    shared_units = shared_gate_up.shape[2]
+    shared_pair = shared_gate_up.reshape(width, 2 * shared_units)
+    both = jnp.dot(both_rows, shared_pair, preferred_element_type=jnp.float32)
+    shared_hidden = (jax.nn.silu(both[:, :shared_units]) * both[:, shared_units:]).astype(
+        jnp.bfloat16
+    )
+    out_cols = jnp.dot(
+        lax.all_gather(shared_hidden, "dp", axis=1, tiled=True),
+        shared_down,
+        preferred_element_type=jnp.float32,
+    )
+    sums = routed.astype(jnp.float32) + out_cols
+    back = lax.all_to_all(sums, "dp", split_axis=0, concat_axis=1, tiled=True)
+    total = resid.astype(jnp.float32) + back
+    return rms_scale(total, final_gain).astype(jnp.bfloat16)
+
+
 def solution(mesh):
     in_specs = (
         P(("dp", "expert"), None),
@@ -109,5 +182,5 @@
     )
     out_specs = P(("dp", "expert"), None)
     return jax.shard_map(
-        per_device, mesh=mesh, in_specs=in_specs, out_specs=out_specs, check_vma=False
+        pair if mesh.shape["dp"] == 2 else general, mesh=mesh, in_specs=in_specs, out_specs=out_specs, check_vma=False
     )

time: 198 us -> 234 us (1.18); the launches traced: 194 us -> 233 us
  waiting for transfers between devices: 97.2 us -> 126 us
  blocking collectives: 28.2 us -> 51.8 us
  starting transfers between devices: 18.9 us -> 4.97 us
    reduce_scatter x0 -> x1, waiting for transfers between devices: none -> 44.8 us  [pair(): lax.psum_scatter(result.astype(jnp.bfloat16), 'expert', scatter_dimension...]
    ppermute x0 -> x1, waiting for transfers between devices: none -> 32.6 us  [pair(): both = own + lax.ppermute(other, 'dp', swap).astype(jnp.float32)]
    all_to_all x4 -> x1, waiting for transfers between devices: 35.4 us -> 4.4 us  [pair(): lax.all_to_all(proj_cols, 'dp', split_axis=0, concat_axis=1, tiled=True)]
    all_gather x2, waiting for transfers between devices: 60.4 us -> 43.7 us  [the longest x1 42.1 us: pair(): every = lax.all_gather(mine, 'expert', axis=0, tiled=True)]
    all_gather x3 -> x5, blocking collectives: 28.2 us -> 44.1 us  [the longest x1 19.5 us: pair(): gates_all = lax.all_gather(gates, 'expert', axis=0, tiled=True)]
    all_to_all x4 -> x1, starting transfers between devices: 18.9 us -> 3.38 us  [pair(): lax.all_to_all(proj_cols, 'dp', split_axis=0, concat_axis=1, tiled=True)]
    all_to_all x0 -> x1, blocking collectives: none -> 7.71 us  [pair(): back = lax.all_to_all(sums, 'dp', split_axis=0, concat_axis=1, tiled=True)]
    add x0 -> x1, other arithmetic: none -> 2.5 us  [pair(): both = own + lax.ppermute(other, 'dp', swap).astype(jnp.float32)]
  transfers between devices with their start and end apart: 6 -> 5, of which waited for: 4 -> 5; matrix products, arithmetic and copies ran while one was open for 16% -> 4% of each run, Pallas kernels for 0% -> 0%
where the time goes in v1:
time: 234 us; the launch traced here: 233 us
  waiting for transfers between devices  126 us (54%)
  blocking collectives  51.8 us (22%)
  matrix products  19.8 us (8%)
  between operations  13.3 us (6%)
  local copies, waits for them, and re-layouts  12.3 us (5%)
  other arithmetic  5.45 us (2%)
  starting transfers between devices  4.97 us (2%)
    reduce_scatter x1, waiting for transfers between devices, pair(): lax.psum_scatter(result.astype(jnp.bfloat16), 'expert', scatter_dimension...  44.8 us
    all_gather x1, waiting for transfers between devices, pair(): every = lax.all_gather(mine, 'expert', axis=0, tiled=True)  42.1 us
    ppermute x1, waiting for transfers between devices, pair(): both = own + lax.ppermute(other, 'dp', swap).astype(jnp.float32)  32.6 us
    all_gather x1, blocking collectives, pair(): gates_all = lax.all_gather(gates, 'expert', axis=0, tiled=True)  19.5 us
    unnamed x19, local copies, waits for them, and re-layouts  10.3 us
    all_to_all x1, blocking collectives, pair(): back = lax.all_to_all(sums, 'dp', split_axis=0, concat_axis=1, tiled=True)  7.71 us
    all_gather x1, blocking collectives, pair(): lax.all_gather(attention_out, 'dp', axis=0, tiled=True)  7.44 us
    all_gather x1, blocking collectives, pair(): lax.all_gather(shared_hidden, 'dp', axis=1, tiled=True)  7.13 us
  transfers between devices with their start and end apart: 5, of which 5 were waited for; matrix products, arithmetic and copies ran while one was open for 4% of the time, Pallas kernels for 0%

profile of v1, /device:TPU:0, one launch (start us, length us, event | category | flops | bytes accessed | tf_op | source)
XLA Modules:
  0.0 233.1 jit_solution(3201300850931685487)
XLA Ops:
  6.5 7.4 %all_gather.21 = bf16[64,2048]{1,0:T(8,128)(2,1)S(1)} all-gather(bf16[32,2048]{1,0:T(8,128)(2,1)} %param.13), channel_id=1, replica_groups=mesh['dp'=2,'expert'=16] {'dp'}, dimensions={0}, use_global_device_ids=true | all-gather | bytes 393216 | tf_op jit(solution)/shard_map/all_gather | solution.py:119
  14.0 3.7 %convolution_convert_fusion = bf16[64,1024]{1,0:T(8,128)(2,1)} fusion(bf16[64,2048]{1,0:T(8,128)(2,1)S(1)} %all_gather.21, bf16[2048,1024]{1,0:T(8,128)(2,1)} %param.14), kind=kOutput, calls=%fused_computation.9 | convolution fusion | flops 268500992 | bytes 4587520 | tf_op jit(solution)/shard_map/dot_general | solution.py:118
  17.7 3.4 %all-to-all-start = ((bf16[2,32,1024]{2,1,0:T(8,128)(2,1)}), bf16[2,32,1024]{2,1,0:T(8,128)(2,1)S(1)}, u32[]{:S(2)}, u32[]{:S(2)}) async-start(bf16[2,32,1024]{2,1,0:T(8,128)(2,1)} %bitcast), calls=%async_computation | async-start | bytes 262144 | tf_op jit(solution)/shard_map/all_to_all | solution.py:123
  21.2 4.4 %all-to-all-done = bf16[2,32,1024]{2,1,0:T(8,128)(2,1)S(1)} async-done(((bf16[2,32,1024]{2,1,0:T(8,128)(2,1)}), bf16[2,32,1024]{2,1,0:T(8,128)(2,1)S(1)}, u32[]{:S(2)}, u32[]{:S(2)}) %all-to-all-start) | async-done | bytes 131104 | tf_op jit(solution)/shard_map/all_to_all | solution.py:123
  25.6 0.2 fusion.6
  25.8 0.1 fusion.8
  25.9 5.6 %all_gather.22 = bf16[64,2048]{1,0:T(8,128)(2,1)S(1)} all-gather(bf16[32,2048]{1,0:T(8,128)(2,1)S(1)} %fusion.8), channel_id=1, replica_groups=mesh['dp'=2,'expert'=16] {'dp'}, dimensions={0}, use_global_device_ids=true | all-gather | bytes 393216 | tf_op jit(solution)/shard_map/all_gather | solution.py:126
  31.5 0.7 constant_dynamic-slice_fusion
  32.3 42.1 %all-gather.5.cloned.1.call-done = bf16[1024,1024]{1,0:T(8,128)(2,1)} async-done(((bf16[64,1024]{1,0:T(8,128)(2,1)}), bf16[1024,1024]{1,0:T(8,128)(2,1)}) %all-gather.5.cloned.1.call-update) | async-done | bytes 2097168 | tf_op jit(solution)/shard_map/all_gather | solution.py:129
  74.3 5.0 %fusion = f32[1024,1408]{1,0:T(8,128)S(1)} fusion(bf16[1024,1024]{1,0:T(8,128)(2,1)} %all-gather.5.cloned.1.call-done, bf16[1,1024,1408]{2,1,0:T(8,128)(2,1)S(1)} %copy-done), kind=kOutput, calls=%fused_computation.1 | convolution fusion | flops 2952790016 | bytes 10747904 | tf_op jit(solution)/shard_map/dot_general | solution.py:139
  79.4 2.5 %copy-done.1 = f32[1024,1408]{1,0:T(8,128)} copy-done((f32[1024,1408]{1,0:T(8,128)}, f32[1024,1408]{1,0:T(8,128)S(1)}, u32[]{:S(2)}) %copy-start.1) | copy-done | bytes 5767192
  81.8 1.3 dynamic-slice_convert_fusion
  83.2 1.5 collective-permute-start
  84.6 32.6 %collective-permute-done = bf16[512,1408]{1,0:T(8,128)(2,1)} collective-permute-done((bf16[512,1408]{1,0:T(8,128)(2,1)}, bf16[512,1408]{1,0:T(8,128)(2,1)}, u32[]{:S(2)}, u32[]{:S(2)}) %collective-permute-start) | collective-permute-done | bytes 1441824 | tf_op jit(solution)/shard_map/ppermute | solution.py:143
  117.2 2.5 %convert_add_fusion = f32[512,1408]{1,0:T(8,128)S(1)} fusion(bf16[512,1408]{1,0:T(8,128)(2,1)} %collective-permute-done, f32[1024,1408]{1,0:T(8,128)} %copy-done.1, s32[]{:T(128)S(6)} %select_n.18), kind=kLoop, calls=%fused_computation.3 | loop fusion | flops 1441792 | bytes 7208964 | tf_op jit(solution)/shard_map/add | solution.py:143
  119.7 1.5 fusion.2
  121.4 4.3 %all-gather = s32[2,32,6]{1,2,0:T(8,128)S(1)} all-gather(s32[1,32,6]{1,2,0:T(8,128)S(1)} %bitcast.41), channel_id=1, replica_groups=mesh['dp'=2,'expert'=16] {'dp'}, dimensions={0}, use_global_device_ids=true | all-gather | bytes 2304 | tf_op jit(solution)/shard_map/all_gather | solution.py:127
  125.8 0.2 fusion.10
  126.1 19.5 %all-gather.1 = f32[16,64,16]{1,2,0:T(8,128)S(1)} all-gather(f32[1,64,16]{1,2,0:T(8,128)S(1)} %divide_bitcast_fusion), channel_id=1, replica_groups=mesh['dp'=2,'expert'=16] {'expert'}, dimensions={0}, use_global_device_ids=true | all-gather | bytes 69632 | tf_op jit(solution)/shard_map/all_gather | solution.py:135
  145.6 0.1 reshape.38
  145.7 0.1 select_reduce_fusion
  145.8 1.6 all-gather.7.cloned.1.call-done
  147.4 5.0 %multiply_convert_fusion = bf16[1024,1024]{1,0:T(8,128)(2,1)} fusion(f32[1024]{0:T(1024)S(1)} %select_reduce_fusion, bf16[1024,704]{1,0:T(8,128)(2,1)} %all-gather.7.cloned.1.call-done, bf16[1,704,1024]{2,1,0:T(8,128)(2,1)} %param.20), kind=kOutput, calls=%fused_computation | convolution fusion | flops 1480589312 | bytes 4984832 | tf_op jit(solution)/shard_map/dot_general | solution.py:146
  152.4 7.6 %copy.31 = bf16[256,8,2,1408]{3,1,2,0:T(8,128)(2,1)S(1)} copy(bf16[256,8,2,1408]{3,2,1,0:T(2,128)(2,1)} %bitcast.35) | data formatting | bytes 23068672
  160.0 2.1 fusion.11
  162.1 0.1 fusion.5
  162.2 7.1 %all_gather.27 = bf16[64,2816]{1,0:T(8,128)(2,1)} all-gather(bf16[64,1408]{1,0:T(8,128)(2,1)S(1)} %fusion.5), channel_id=1, replica_groups=mesh['dp'=2,'expert'=16] {'dp'}, dimensions={1}, use_global_device_ids=true | all-gather | bytes 540672 | tf_op jit(solution)/shard_map/all_gather | solution.py:158
  169.3 44.8 %reduce-scatter.2.cloned.1.call-done = bf16[64,1024]{1,0:T(8,128)(2,1)} async-done(((bf16[1024,1024]{1,0:T(8,128)(2,1)}), bf16[64,1024]{1,0:T(8,128)(2,1)}) %reduce-scatter.2.cloned.1.call-update) | async-done | bytes 131088 | tf_op jit(solution)/shard_map/reduce_scatter | solution.py:148
  214.1 3.8 %convolution_add_fusion = f32[64,1024]{1,0:T(8,128)S(1)} fusion(bf16[64,2816]{1,0:T(8,128)(2,1)} %all_gather.27, bf16[2816,1024]{1,0:T(8,128)(2,1)} %param.22, bf16[64,1024]{1,0:T(8,128)(2,1)} %reduce-scatter.2.cloned.1.call-done), kind=kOutput, calls=%fused_computation.8 | convolution fusion | flops 369229824 | bytes 6520832 | tf_op jit(solution)/shard_map/dot_general | solution.py:157
  217.9 7.7 %all_to_all.32 = f32[2,32,1024]{2,1,0:T(8,128)S(1)} all-to-all(f32[2,32,1024]{2,1,0:T(8,128)S(1)} %bitcast.38), channel_id=1, replica_groups=mesh['dp'=2,'expert'=16] {'dp'}, dimensions={0} | all-to-all | bytes 524288 | tf_op jit(solution)/shard_map/all_to_all | solution.py:163
  225.7 0.1 multiply_reduce_fusion
  225.8 0.8 multiply_convert_fusion.1
  (32 shorter events, 0.4 us)
Async XLA Ops:
  6.5 67.8 %copy-start = (bf16[1,1024,1408]{2,1,0:T(8,128)(2,1)S(1)}, bf16[1,1024,1408]{2,1,0:T(8,128)(2,1)}, u32[]{:S(2)}) copy-start(bf16[1,1024,1408]{2,1,0:T(8,128)(2,1)} %param.19) | copy-start | bytes 8650756
  14.0 11.6 %copy-start.2 = (bf16[32,2048]{1,0:T(8,128)(2,1)S(1)}, bf16[32,2048]{1,0:T(8,128)(2,1)}, u32[]{:S(2)}) copy-start(bf16[32,2048]{1,0:T(8,128)(2,1)} %param.12) | copy-start | bytes 393220
  14.0 11.8 %copy-start.5 = (f32[2048]{0:T(1024)S(1)}, f32[2048]{0:T(1024)}, u32[]{:S(2)}) copy-start(f32[2048]{0:T(1024)} %param.15) | copy-start | bytes 24580
  17.7 7.8 %all-to-all-start = ((bf16[2,32,1024]{2,1,0:T(8,128)(2,1)}), bf16[2,32,1024]{2,1,0:T(8,128)(2,1)S(1)}, u32[]{:S(2)}, u32[]{:S(2)}) async-start(bf16[2,32,1024]{2,1,0:T(8,128)(2,1)} %bitcast), calls=%async_computation | async-start | bytes 262144 | tf_op jit(solution)/shard_map/all_to_all | solution.py:123
  21.1 53.2 %all-gather.5.cloned.1.call-start = ((), (), s32[]{:S(2)}) async-start(), calls=%async_computation.3 | async-start | bytes 2228224 | tf_op jit(solution)/shard_map/all_gather | solution.py:129
  32.2 115.2 %all-gather.7.cloned.1.call-start = ((), (), s32[]{:S(2)}) async-start(), calls=%async_computation.4 | async-start | bytes 2359296 | tf_op jit(solution)/shard_map/all_gather | solution.py:145
  79.4 2.5 %copy-start.1 = (f32[1024,1408]{1,0:T(8,128)}, f32[1024,1408]{1,0:T(8,128)S(1)}, u32[]{:S(2)}) copy-start(f32[1024,1408]{1,0:T(8,128)S(1)} %fusion) | copy-start | bytes 17301508
  83.2 34.1 %collective-permute-start = (bf16[512,1408]{1,0:T(8,128)(2,1)}, bf16[512,1408]{1,0:T(8,128)(2,1)}, u32[]{:S(2)}, u32[]{:S(2)}) collective-permute-start(bf16[512,1408]{1,0:T(8,128)(2,1)} %dynamic-slice_convert_fusion), channel_id=1, source_target_pairs={{0,16},{16,0},{1,17},{17,1},{2,18},{18,2},{3,19},{19,3},{4,20},{20... | collective-permute-start | bytes 4325384 | tf_op jit(solution)/shard_map/ppermute | solution.py:143
  119.7 1.7 copy-start.6
  119.7 6.1 %copy-start.7 = (s32[16]{0:T(128)S(1)}, s32[16]{0:T(128)}, u32[]{:S(2)}) copy-start(s32[16]{0:T(128)} %param.18) | copy-start | bytes 196
  119.7 6.1 %copy-start.3 = (bf16[2048,16]{0,1:T(8,128)(2,1)S(1)}, bf16[2048,16]{0,1:T(8,128)(2,1)}, u32[]{:S(2)}) copy-start(bf16[2048,16]{0,1:T(8,128)(2,1)} %param.16) | copy-start | bytes 196612
  121.3 92.8 %reduce-scatter.2.cloned.1.call-start = ((), (), s32[]{:S(2)}) async-start(), calls=%async_computation.5 | async-start | bytes 2228224 | tf_op jit(solution)/shard_map/reduce_scatter | solution.py:148
  169.3 56.5 %copy-start.4 = (f32[2048]{0:T(1024)S(1)}, f32[2048]{0:T(1024)}, u32[]{:S(2)}) copy-start(f32[2048]{0:T(1024)} %param.23) | copy-start | bytes 24580
Sparse Core Ops, SparseCore 0:
  32.3 41.9 all-gather.4
  121.4 25.9 all-gather.6
  152.5 61.5 reduce-scatter.1

commit v2 on v1

--- a/solution.py
+++ b/solution.py
@@ -1,6 +1,10 @@
+import functools
+
 import jax
 import jax.numpy as jnp
 from jax import lax
+from jax.experimental import pallas as pl
+from jax.experimental.pallas import tpu as pltpu
 from jax.sharding import PartitionSpec as P
 
 EPS = 1e-06
@@ -95,6 +99,279 @@
     return rms_scale(total, final_gain).astype(jnp.bfloat16)
 
 
+GROUPS = 4
+
+
+def routed_kernel(
+    cap,
+    block_ref,
+    gate_up_ref,
+    down_ref,
+    out_ref,
+    gath,
+    own_part,
+    part_send,
+    part_recv,
+    act_send,
+    act_recv,
+    con,
+    core_send,
+    core_recv,
+    keep,
+    y_send,
+    y_recv,
+    z_send,
+    z_recv,
+    gz_s,
+    gz_r,
+    gy_s,
+    gy_r,
+    gc_s,
+    gc_r,
+    p_s,
+    p_r,
+    a_s,
+    a_r,
+    c_s,
+    c_r,
+    y_s,
+    y_r,
+    z_s,
+    z_r,
+):
+    d = lax.axis_index("dp")
+    e = lax.axis_index("expert")
+    z, y, c = e // 4, (e // 2) % 2, e % 2
+    half = gate_up_ref.shape[0]
+    units = down_ref.shape[0]
+    pair_rows = block_ref.shape[0]
+    span = 2 * pair_rows
+    taken = 4 * cap
+    experts = 16
+
+    def place(zz, yy, cc):
+        return zz * 4 + yy * 2 + cc
+
+    x_peer = (1 - d, e)
+    y_peer = (d, place(z, 1 - y, c))
+    c_peer = (d, place(z, y, 1 - c))
+
+    def z_peer(dz):
+        return (d, place((z + dz) % GROUPS, y, c))
+
+    def copy(src, dst, send, recv, device):
+        return pltpu.make_async_remote_copy(
+            src_ref=src,
+            dst_ref=dst,
+            send_sem=send,
+            recv_sem=recv,
+            device_id=device,
+            device_id_type=pl.DeviceIdType.MESH,
+        )
+
+    barrier = pltpu.get_barrier_semaphore()
+    peers = [x_peer, y_peer, c_peer] + [z_peer(k) for k in range(1, GROUPS)]
+    for peer in peers:
+        pl.semaphore_signal(
+            barrier, inc=1, device_id=peer, device_id_type=pl.DeviceIdType.MESH
+        )
+    gath[z, y, c] = block_ref[...]
+    pl.semaphore_wait(barrier, len(peers))
+
+    started = []
+
+    def go(cp):
+        cp.start()
+        started.append(cp)
+
+    def source(dz):
+        return (z + GROUPS - dz) % GROUPS
+
+    def gather_z(dz):
+        return copy(
+            gath.at[z, y, c], gath.at[z, y, c], gz_s.at[dz], gz_r.at[dz], z_peer(dz)
+        )
+
+    def send_yc(dz):
+        held = gath.at[source(dz), y, c]
+        go(copy(held, held, gy_s.at[dz], gy_r.at[dz], y_peer))
+        go(copy(held, held, gc_s.at[dz, 0], gc_r.at[dz, 0], c_peer))
+
+    def landed(slot, recv):
+        copy(slot, slot, gz_s.at[0], recv, x_peer).wait_recv()
+
+    def first():
+        for dz in (1, 3, 2):
+            go(gather_z(dz))
+        send_yc(0)
+
+    def arrive_z(dz):
+        landed(gath.at[source(dz), y, c], gz_r.at[dz])
+        send_yc(dz)
+
+    def arrive(dz):
+        far = gath.at[source(dz), 1 - y, c]
+        landed(far, gy_r.at[dz])
+        go(copy(far, far, gc_s.at[dz, 1], gc_r.at[dz, 1], c_peer))
+        landed(gath.at[source(dz), y, 1 - c], gc_r.at[dz, 0])
+        landed(gath.at[source(dz), 1 - y, 1 - c], gc_r.at[dz, 1])
+
+    def facts(dz, h):
+        lane = lax.broadcasted_iota(jnp.int32, (span, 128), 1)
+        aux = gath[source(dz), h, :, :, pl.ds(half, 128)].reshape(span, 128)
+        aux = aux.astype(jnp.float32)
+        code = jnp.sum(jnp.where(lane == e, aux, 0.0), axis=1, keepdims=True)
+        upper = jnp.where(lane == e + experts, aux, 0.0)
+        lower = jnp.where(lane == e + 2 * experts, aux, 0.0)
+        gate = jnp.sum(upper + lower, axis=1, keepdims=True)
+        row = lax.broadcasted_iota(jnp.int32, (span, taken), 0)
+        start = (row // (pair_rows // 2)) * cap
+        slot = lax.broadcasted_iota(jnp.int32, (span, taken), 1)
+        code = code.astype(jnp.int32)
+        hit = (code > 0) & (slot - start == code - 1)
+        return jnp.where(hit, 1.0, 0.0).astype(jnp.bfloat16), gate
+
+    def partial(dz, h):
+        select, _ = facts(dz, h)
+        rows = gath[source(dz), h, :, :, pl.ds(0, half)].reshape(span, half)
+        packed = lax.dot_general(
+            select, rows, (((0,), (0,)), ((), ())), preferred_element_type=jnp.float32
+        ).astype(jnp.bfloat16)
+        return jnp.dot(packed, gate_up_ref[...], preferred_element_type=jnp.float32)
+
+    def stage_a(dz):
+        part_send[dz] = partial(dz, 1 - d).astype(jnp.bfloat16)
+        go(copy(part_send.at[dz], part_recv.at[dz], p_s.at[dz], p_r.at[dz], x_peer))
+        own_part[dz] = partial(dz, d)
+
+    def stage_b(dz):
+        landed(part_recv.at[dz], p_r.at[dz])
+        both = own_part[dz] + part_recv[dz].astype(jnp.float32)
+        gate, up = both[:, :units], both[:, units:]
+        act_send[dz] = (gate / (1.0 + jnp.exp(-gate)) * up).astype(jnp.bfloat16)
+        go(copy(act_send.at[dz], act_recv.at[dz], a_s.at[dz], a_r.at[dz], x_peer))
+        spread(dz, 0, d, act_send)
+
+    def spread(dz, i, h, held):
+        select, gate = facts(dz, h)
+        result = jnp.dot(held[dz], down_ref[...], preferred_element_type=jnp.float32)
+        result = result.astype(jnp.bfloat16)
+        con[...] = gate * jnp.dot(select, result, preferred_element_type=jnp.float32)
+        core_send[dz, i] = con[pl.ds((1 - c) * pair_rows, pair_rows), :].astype(jnp.bfloat16)
+        go(
+            copy(
+                core_send.at[dz, i], core_recv.at[dz, i], c_s.at[dz, i], c_r.at[dz, i], c_peer
+            )
+        )
+        keep[dz, i] = con[pl.ds(c * pair_rows, pair_rows), :]
+
+    def stage_c(dz):
+        landed(act_recv.at[dz], a_r.at[dz])
+        spread(dz, 1, 1 - d, act_recv)
+
+    near = (d + y) % 2
+
+    def stage_r1(dz):
+        for i in range(2):
+            landed(core_recv.at[dz, i], c_r.at[dz, i])
+        away = keep[dz, 1 - near] + core_recv[dz, 1 - near].astype(jnp.float32)
+        y_send[dz] = away.astype(jnp.bfloat16)
+        go(copy(y_send.at[dz], y_recv.at[dz], y_s.at[dz], y_r.at[dz], y_peer))
+
+    def stage_r2(dz):
+        landed(y_recv.at[dz], y_r.at[dz])
+        mine = keep[dz, near] + core_recv[dz, near].astype(jnp.float32)
+        mine = mine + y_recv[dz].astype(jnp.float32)
+        if dz == 0:
+            out_ref[...] = mine
+        else:
+            z_send[dz] = mine.astype(jnp.bfloat16)
+            go(
+                copy(
+                    z_send.at[dz], z_recv.at[dz], z_s.at[dz], z_r.at[dz], z_peer(GROUPS - dz)
+                )
+            )
+
+    first()
+    arrive(0)
+    stage_a(0)
+    arrive_z(1)
+    arrive_z(3)
+    arrive(1)
+    stage_a(1)
+    arrive_z(2)
+    arrive(3)
+    stage_a(3)
+    stage_b(0)
+    arrive(2)
+    stage_a(2)
+    stage_b(1)
+    stage_c(0)
+    stage_r1(0)
+    stage_b(3)
+    stage_c(1)
+    stage_r2(0)
+    stage_r1(1)
+    stage_b(2)
+    stage_c(3)
+    stage_r2(1)
+    stage_r1(3)
+    stage_c(2)
+    stage_r1(2)
+    stage_r2(3)
+    stage_r2(2)
+    for dz in (1, 3, 2):
+        landed(z_recv.at[dz], z_r.at[dz])
+        out_ref[...] += z_recv[dz].astype(jnp.float32)
+    for cp in started:
+        cp.wait_send()
+
+
+def routed_sum(block, gate_up, down, cap):
+    pair_rows, wide = block.shape
+    half, both = gate_up.shape
+    units, cols = down.shape
+    taken = 4 * cap
+    bf, f32 = jnp.bfloat16, jnp.float32
+    dma = pltpu.SemaphoreType.DMA
+    vmem = pl.BlockSpec(memory_space=pltpu.VMEM)
+    return pl.pallas_call(
+        functools.partial(routed_kernel, cap),
+        out_shape=jax.ShapeDtypeStruct((pair_rows, cols), f32),
+        in_specs=[vmem] * 3,
+        out_specs=vmem,
+        scratch_shapes=[
+            pltpu.VMEM((4, 2, 2, pair_rows, wide), bf),
+            pltpu.VMEM((4, taken, both), f32),
+            pltpu.VMEM((4, taken, both), bf),
+            pltpu.VMEM((4, taken, both), bf),
+            pltpu.VMEM((4, taken, units), bf),
+            pltpu.VMEM((4, taken, units), bf),
+            pltpu.VMEM((2 * pair_rows, cols), f32),
+            pltpu.VMEM((4, 2, pair_rows, cols), bf),
+            pltpu.VMEM((4, 2, pair_rows, cols), bf),
+            pltpu.VMEM((4, 2, pair_rows, cols), f32),
+            pltpu.VMEM((4, pair_rows, cols), bf),
+            pltpu.VMEM((4, pair_rows, cols), bf),
+            pltpu.VMEM((4, pair_rows, cols), bf),
+            pltpu.VMEM((4, pair_rows, cols), bf),
+        ]
+        + [dma((4,))] * 4
+        + [dma((4, 2))] * 2
+        + [dma((4,))] * 4
+        + [dma((4, 2))] * 2
+        + [dma((4,))] * 4,
+        compiler_params=pltpu.CompilerParams(
+            collective_id=0, has_side_effects=True, vmem_limit_bytes=48 * 2**20
+        ),
+        cost_estimate=pl.CostEstimate(
+            flops=2 * 16 * pair_rows * half * both * 2,
+            bytes_accessed=2 * (half * both + units * cols),
+            transcendentals=0,
+        ),
+    )(block, gate_up, down)
+
+
 def pair(
     residual_in,
     attention_out,
@@ -109,11 +386,11 @@
     shared_down,
     final_gain,
 ):
-    swap = [(0, 1), (1, 0)]
     d = lax.axis_index("dp")
-    e = lax.axis_index("expert")
     rows, width = residual_in.shape
     experts = router_weight.shape[1]
+    choose = expert_ids.shape[1]
+    cap = max(2, min(rows, 2 * rows * choose // experts))
     half = width // 2
     proj_cols = jnp.dot(
         lax.all_gather(attention_out, "dp", axis=0, tiled=True),
@@ -123,31 +400,29 @@
     proj = lax.all_to_all(proj_cols, "dp", split_axis=0, concat_axis=1, tiled=True)
     resid = (residual_in.astype(jnp.float32) + proj.astype(jnp.float32)).astype(jnp.bfloat16)
     normed = rms_scale(resid, post_gain).astype(jnp.bfloat16)
-    both_rows = lax.all_gather(normed, "dp", axis=0, tiled=True)
-    ids = lax.all_gather(expert_ids, "dp", axis=0, tiled=True)
-    mine = lax.dynamic_slice_in_dim(both_rows, d * half, half, axis=1)
-    every = lax.all_gather(mine, "expert", axis=0, tiled=True)
-    logits = jnp.dot(both_rows, router_weight, preferred_element_type=jnp.float32)
+    logits = jnp.dot(normed, router_weight, preferred_element_type=jnp.float32)
     expert_range = jnp.arange(experts, dtype=jnp.int32)
-    named = jnp.any(ids[:, :, None] == expert_range[None, None, :], axis=1)
+    to_slot = expert_slot[:, None] == expert_range[None, :]
+    named = jnp.any(expert_ids[:, :, None] == expert_range[None, None, :], axis=1)
     raised = jnp.where(named, jnp.exp(logits), 0.0)
     gates = raised / jnp.sum(raised, axis=1, keepdims=True)
-    gates_all = lax.all_gather(gates, "expert", axis=0, tiled=True)
-    here = (expert_slot == e)[None, :]
-    gate = jnp.sum(jnp.where(here, gates_all, 0.0), axis=1, keepdims=True)
-    units = expert_gate_up.shape[2] // 2
-    part = jnp.dot(every, expert_gate_up[0], preferred_element_type=jnp.float32)
-    count = part.shape[0] // 2
-    other = lax.dynamic_slice_in_dim(part, (1 - d) * count, count).astype(jnp.bfloat16)
-    own = lax.dynamic_slice_in_dim(part, d * count, count)
-    both = own + lax.ppermute(other, "dp", swap).astype(jnp.float32)
-    active = (jax.nn.silu(both[:, :units]) * both[:, units:]).astype(jnp.bfloat16)
-    active = lax.all_gather(active, "dp", axis=0, tiled=True)
-    result = jnp.dot(active, expert_down[0], preferred_element_type=jnp.float32)
-    result = result.astype(jnp.bfloat16).astype(jnp.float32) * gate
-    routed = lax.psum_scatter(
-        result.astype(jnp.bfloat16), "expert", scatter_dimension=0, tiled=True
-    )
+    gates = jnp.sum(jnp.where(to_slot[None], gates[:, :, None], 0.0), axis=1)
+    named = jnp.any(named[:, :, None] & to_slot[None], axis=1)
+    order = jnp.arange(rows, dtype=jnp.int32)
+    upto = (order[:, None] >= order[None, :]).astype(jnp.bfloat16)
+    code = jnp.dot(upto, named.astype(jnp.bfloat16), preferred_element_type=jnp.float32)
+    code = jnp.where(named, code, 0.0)
+    upper = lax.reduce_precision(gates, exponent_bits=8, mantissa_bits=7)
+    aux = jnp.concatenate(
+        [code, upper, gates - upper, jnp.zeros((rows, 128 - 3 * experts), jnp.float32)], axis=1
+    ).astype(jnp.bfloat16)
+    everything = lax.all_gather(
+        jnp.concatenate([normed, aux], axis=1), "dp", axis=0, tiled=True
+    )
+    both_rows = everything[:, :width]
+    mine = lax.dynamic_slice_in_dim(everything, d * half, half, axis=1)
+    block = jnp.concatenate([mine, everything[:, width:]], axis=1)
+    routed = routed_sum(block, expert_gate_up[0], expert_down[0], cap)
     shared_units = shared_gate_up.shape[2]
     shared_pair = shared_gate_up.reshape(width, 2 * shared_units)
     both = jnp.dot(both_rows, shared_pair, preferred_element_type=jnp.float32)
@@ -159,8 +434,7 @@
         shared_down,
         preferred_element_type=jnp.float32,
     )
-    sums = routed.astype(jnp.float32) + out_cols
-    back = lax.all_to_all(sums, "dp", split_axis=0, concat_axis=1, tiled=True)
+    back = lax.all_to_all(routed + out_cols, "dp", split_axis=0, concat_axis=1, tiled=True)
     total = resid.astype(jnp.float32) + back
     return rms_scale(total, final_gain).astype(jnp.bfloat16)
 
@@ -182,5 +456,5 @@
     )
     out_specs = P(("dp", "expert"), None)
     return jax.shard_map(
-        pair if mesh.shape["dp"] == 2 else general, mesh=mesh, in_specs=in_specs, out_specs=out_specs, check_vma=False
-    )
+        pair if dict(mesh.shape) == {"dp": 2, "expert": 16} else general, mesh=mesh, in_specs=in_specs, out_specs=out_specs, check_vma=False
+    )

time: 234 us -> 126 us (0.54)
  waiting for transfers between devices: 126 us -> 0.01 us
  Pallas kernels: 0 us -> 67.5 us
  blocking collectives: 51.8 us -> 27.7 us
  between operations: 13.3 us -> 0.23 us
  matrix products: 19.8 us -> 11.7 us
  other arithmetic: 5.45 us -> 3.06 us
    pallas_call x0 -> x1, Pallas kernels: none -> 67.5 us  [routed_sum(): pl.pallas_call(functools.partial(routed_kernel, cap), out_shape=jax.Shape...]
    reduce_scatter x1 -> x0, waiting for transfers between devices: 44.8 us -> none  [pair(): lax.psum_scatter(result.astype(jnp.bfloat16), 'expert', scatter_dimension...]
    all_gather x2 -> x0, waiting for transfers between devices: 43.7 us -> none  [the longest x1 42.1 us: pair(): every = lax.all_gather(mine, 'expert', axis=0, tiled=True)]
    ppermute x1 -> x0, waiting for transfers between devices: 32.6 us -> none  [pair(): both = own + lax.ppermute(other, 'dp', swap).astype(jnp.float32)]
    all_gather x3 -> x1, blocking collectives: 29.5 us -> 5.73 us  [pair(): lax.all_gather(jnp.concatenate([normed, aux], axis=1), 'dp', axis=0, tile...]
    dot_general x3 -> x2, matrix products: 10.2 us -> 0.4 us  [the longest x1 0.27 us: pair(): logits = jnp.dot(normed, router_weight, preferred_element_type=jnp.float32)]
    dot_general x1, matrix products: 2.08 us -> 6.54 us  [pair(): both = jnp.dot(both_rows, shared_pair, preferred_element_type=jnp.float32)]
    all_to_all x1, waiting for transfers between devices: 4.4 us -> 0.01 us  [pair(): lax.all_to_all(proj_cols, 'dp', split_axis=0, concat_axis=1, tiled=True)]
  transfers between devices with their start and end apart: 5 -> 1, of which waited for: 5 -> 0; matrix products, arithmetic and copies ran while one was open for 4% -> 10% of each run, Pallas kernels for 0% -> 0%
where the time goes in v2:
time: 126 us
  Pallas kernels  67.5 us (54%)
  blocking collectives  27.7 us (22%)
  local copies, waits for them, and re-layouts  11.9 us (9%)
  matrix products  11.7 us (9%)
  starting transfers between devices  3.38 us (3%)
  other arithmetic  3.06 us (2%)
    pallas_call x1, Pallas kernels, routed_sum(): pl.pallas_call(functools.partial(routed_kernel, cap), out_shape=jax.Shape...  67.5 us
    unnamed x17, local copies, waits for them, and re-layouts  11.4 us
    all_to_all x1, blocking collectives, pair(): lax.all_to_all(routed + out_cols, 'dp', split_axis=0, concat_axis=1, tile...  8.05 us
    all_gather x1, blocking collectives, pair(): lax.all_gather(attention_out, 'dp', axis=0, tiled=True)  7.48 us
    dot_general x1, matrix products, pair(): both = jnp.dot(both_rows, shared_pair, preferred_element_type=jnp.float32)  6.54 us
    all_gather x1, blocking collectives, pair(): lax.all_gather(shared_hidden, 'dp', axis=1, tiled=True)  6.48 us
    all_gather x1, blocking collectives, pair(): lax.all_gather(jnp.concatenate([normed, aux], axis=1), 'dp', axis=0, tile...  5.73 us
    dot_general x1, matrix products, pair(): jnp.dot(lax.all_gather(attention_out, 'dp', axis=0, tiled=True), out_weig...  3.69 us
  transfers between devices with their start and end apart: 1, of which 0 were waited for; matrix products, arithmetic and copies ran while one was open for 10% of the time, Pallas kernels for 0%

profile of v2, /device:TPU:0, one launch (start us, length us, event | category | flops | bytes accessed | tf_op | source)
XLA Modules:
  0.0 125.6 jit_solution(9323379065683399955)
XLA Ops:
  0.0 7.5 %all_gather.9 = bf16[64,2048]{1,0:T(8,128)(2,1)S(1)} all-gather(bf16[32,2048]{1,0:T(8,128)(2,1)} %param.13), channel_id=1, replica_groups=mesh['dp'=2,'expert'=16] {'dp'}, dimensions={0}, use_global_device_ids=true | all-gather | bytes 393216 | tf_op jit(solution)/shard_map/all_gather | solution.py:396
  7.5 3.7 %convolution_convert_fusion = bf16[64,1024]{1,0:T(8,128)(2,1)} fusion(bf16[64,2048]{1,0:T(8,128)(2,1)S(1)} %all_gather.9, bf16[2048,1024]{1,0:T(8,128)(2,1)} %param.14), kind=kOutput, calls=%fused_computation.1 | convolution fusion | flops 268500992 | bytes 4587520 | tf_op jit(solution)/shard_map/dot_general | solution.py:395
  11.2 3.4 %all-to-all-start = ((bf16[2,32,1024]{2,1,0:T(8,128)(2,1)}), bf16[2,32,1024]{2,1,0:T(8,128)(2,1)S(1)}, u32[]{:S(2)}, u32[]{:S(2)}) async-start(bf16[2,32,1024]{2,1,0:T(8,128)(2,1)} %bitcast), calls=%async_computation | async-start | bytes 262144 | tf_op jit(solution)/shard_map/all_to_all | solution.py:400
  14.6 0.7 fusion.8
  15.3 0.7 iota_compare_fusion.3
  16.0 0.1 and_reduce_fusion
  16.1 0.1 copy.33
  16.2 0.1 fusion.1
  16.3 0.1 copy.36
  16.4 0.0 copy-start.5
  16.4 11.3 %copy.47 = bf16[256,8,2,1408]{3,1,2,0:T(8,128)(2,1)} copy(bf16[256,8,2,1408]{3,2,1,0:T(2,128)(2,1)} %bitcast.24) | data formatting | bytes 23068672
  27.8 0.2 fusion.3
  28.0 0.1 fusion.5
  28.1 0.3 fusion.9
  28.4 0.1 broadcast_divide_fusion
  28.4 0.1 copy.38
  28.5 0.1 select_reduce_fusion
  28.6 0.1 copy.40
  28.7 0.1 copy.39
  28.8 0.1 concatenate.9
  28.9 5.7 %all_gather.10 = bf16[64,2176]{1,0:T(8,128)(2,1)S(1)} all-gather(bf16[32,2176]{1,0:T(8,128)(2,1)S(1)} %concatenate.9), channel_id=1, replica_groups=mesh['dp'=2,'expert'=16] {'dp'}, dimensions={0}, use_global_device_ids=true | all-gather | bytes 417792 | tf_op jit(solution)/shard_map/all_gather | solution.py:419
  34.7 0.0 copy-start.1
  34.7 6.5 %fusion.6 = f32[64,2816]{1,0:T(8,128)S(1)} fusion(bf16[2048,2816]{1,0:T(8,128)(2,1)} %bitcast.23, bf16[64,2176]{1,0:T(8,128)(2,1)S(1)} %all_gather.10), kind=kOutput, calls=%fused_computation.14 | convolution fusion | flops 738197504 | bytes 12517376 | tf_op jit(solution)/shard_map/dot_general | solution.py:428
  41.2 0.1 fusion.2
  41.4 0.0 slice-start
  41.4 6.5 %all_gather.11 = bf16[64,2816]{1,0:T(8,128)(2,1)S(1)} all-gather(bf16[64,1408]{1,0:T(8,128)(2,1)S(1)} %fusion.2), channel_id=1, replica_groups=mesh['dp'=2,'expert'=16] {'dp'}, dimensions={1}, use_global_device_ids=true | all-gather | bytes 540672 | tf_op jit(solution)/shard_map/all_gather | solution.py:433
  47.9 0.0 slice-start.1
  47.9 67.5 %shard_map.118 = f32[64,1024]{1,0:T(8,128)S(1)} custom-call(bf16[64,1152]{1,0:T(8,128)(2,1)S(1)} %pad_maximum_fusion.block_ref, bf16[1024,1408]{1,0:T(8,128)(2,1)S(1)} %bitcast.21, bf16[704,1024]{1,0:T(8,128)(2,1)S(1)} %bitcast.22), custom_call_target="tpu_custom_call" | custom-call | flops 5905580032 | bytes 4325376 | tf_op jit(solution)/shard_map/pallas_call | solution.py:338
  115.5 1.1 convolution_add_fusion
  116.6 8.0 %all_to_all.32 = f32[2,32,1024]{2,1,0:T(8,128)S(1)} all-to-all(f32[2,32,1024]{2,1,0:T(8,128)S(1)} %bitcast.29), channel_id=1, replica_groups=mesh['dp'=2,'expert'=16] {'dp'}, dimensions={0} | all-to-all | bytes 524288 | tf_op jit(solution)/shard_map/all_to_all | solution.py:437
  124.7 0.2 multiply_reduce_fusion
  124.8 0.8 multiply_convert_fusion
  (25 shorter events, 0.1 us)
Async XLA Ops:
  0.0 28.1 %copy-start = (bf16[2048,16]{0,1:T(8,128)(2,1)S(1)}, bf16[2048,16]{0,1:T(8,128)(2,1)}, u32[]{:S(2)}) copy-start(bf16[2048,16]{0,1:T(8,128)(2,1)} %param.16) | copy-start | bytes 196612
  11.2 16.6 %all-to-all-start = ((bf16[2,32,1024]{2,1,0:T(8,128)(2,1)}), bf16[2,32,1024]{2,1,0:T(8,128)(2,1)S(1)}, u32[]{:S(2)}, u32[]{:S(2)}) async-start(bf16[2,32,1024]{2,1,0:T(8,128)(2,1)} %bitcast), calls=%async_computation | async-start | bytes 262144 | tf_op jit(solution)/shard_map/all_to_all | solution.py:400
  16.4 11.4 %copy-start.3 = (bf16[32,2048]{1,0:T(8,128)(2,1)S(1)}, bf16[32,2048]{1,0:T(8,128)(2,1)}, u32[]{:S(2)}) copy-start(bf16[32,2048]{1,0:T(8,128)(2,1)} %param.12) | copy-start | bytes 393220
  16.4 11.6 %copy-start.5 = (f32[2048]{0:T(1024)S(1)}, f32[2048]{0:T(1024)}, u32[]{:S(2)}) copy-start(f32[2048]{0:T(1024)} %param.15) | copy-start | bytes 24580
  34.7 13.2 %copy-start.1 = (bf16[1,1024,1408]{2,1,0:T(8,128)(2,1)S(1)}, bf16[1,1024,1408]{2,1,0:T(8,128)(2,1)}, u32[]{:S(2)}) copy-start(bf16[1,1024,1408]{2,1,0:T(8,128)(2,1)} %param.19) | copy-start | bytes 8650756
  34.7 13.2 %copy-start.2 = (bf16[1,704,1024]{2,1,0:T(8,128)(2,1)S(1)}, bf16[1,704,1024]{2,1,0:T(8,128)(2,1)}, u32[]{:S(2)}) copy-start(bf16[1,704,1024]{2,1,0:T(8,128)(2,1)} %param.20) | copy-start | bytes 4325380
  41.4 74.1 %slice-start = ((s8[5767168]{0:T(1024)(128)(4,1)}), s8[4194304]{0:T(1024)(128)(4,1)S(1)}, s32[]{:S(2)}) async-start(s8[5767168]{0:T(1024)(128)(4,1)} %bitcast.25), calls=%async_computation.2 | async-start | bytes 8388608
  47.9 67.6 %slice-start.1 = ((s8[5767168]{0:T(1024)(128)(4,1)}), s8[1572864]{0:T(1024)(128)(4,1)S(1)}, s32[]{:S(2)}) async-start(s8[5767168]{0:T(1024)(128)(4,1)} %bitcast.25), calls=%async_computation.3 | async-start | bytes 3145728
  115.5 9.4 %copy-start.4 = (f32[2048]{0:T(1024)S(1)}, f32[2048]{0:T(1024)}, u32[]{:S(2)}) copy-start(f32[2048]{0:T(1024)} %param.23) | copy-start | bytes 24580

commit v3 on v2

--- a/solution.py
+++ b/solution.py
@@ -107,7 +107,10 @@
     block_ref,
     gate_up_ref,
     down_ref,
+    hidden_ref,
     out_ref,
+    hidden_out,
+    hidden_recv,
     gath,
     own_part,
     part_send,
@@ -138,6 +141,8 @@
     y_r,
     z_s,
     z_r,
+    h_s,
+    h_r,
 ):
     d = lax.axis_index("dp")
     e = lax.axis_index("expert")
@@ -293,6 +298,7 @@
             )
 
     first()
+    go(copy(hidden_ref, hidden_recv, h_s.at[0], h_r.at[0], x_peer))
     arrive(0)
     stage_a(0)
     arrive_z(1)
@@ -323,11 +329,14 @@
     for dz in (1, 3, 2):
         landed(z_recv.at[dz], z_r.at[dz])
         out_ref[...] += z_recv[dz].astype(jnp.float32)
+    landed(hidden_recv, h_r.at[0])
+    hidden_out[d] = hidden_ref[...]
+    hidden_out[1 - d] = hidden_recv[...]
     for cp in started:
         cp.wait_send()
 
 
-def routed_sum(block, gate_up, down, cap):
+def routed_sum(block, gate_up, down, hidden, cap):
     pair_rows, wide = block.shape
     half, both = gate_up.shape
     units, cols = down.shape
@@ -337,10 +346,14 @@
     vmem = pl.BlockSpec(memory_space=pltpu.VMEM)
     return pl.pallas_call(
         functools.partial(routed_kernel, cap),
-        out_shape=jax.ShapeDtypeStruct((pair_rows, cols), f32),
-        in_specs=[vmem] * 3,
-        out_specs=vmem,
+        out_shape=(
+            jax.ShapeDtypeStruct((pair_rows, cols), f32),
+            jax.ShapeDtypeStruct((2, *hidden.shape), bf),
+        ),
+        in_specs=[vmem] * 4,
+        out_specs=(vmem, vmem),
         scratch_shapes=[
+            pltpu.VMEM(hidden.shape, bf),
             pltpu.VMEM((4, 2, 2, pair_rows, wide), bf),
             pltpu.VMEM((4, taken, both), f32),
             pltpu.VMEM((4, taken, both), bf),
@@ -360,7 +373,8 @@
         + [dma((4, 2))] * 2
         + [dma((4,))] * 4
         + [dma((4, 2))] * 2
-        + [dma((4,))] * 4,
+        + [dma((4,))] * 4
+        + [dma((1,))] * 2,
         compiler_params=pltpu.CompilerParams(
             collective_id=0, has_side_effects=True, vmem_limit_bytes=48 * 2**20
         ),
@@ -369,7 +383,7 @@
             bytes_accessed=2 * (half * both + units * cols),
             transcendentals=0,
         ),
-    )(block, gate_up, down)
+    )(block, gate_up, down, hidden)
 
 
 def pair(
@@ -422,20 +436,20 @@
     both_rows = everything[:, :width]
     mine = lax.dynamic_slice_in_dim(everything, d * half, half, axis=1)
     block = jnp.concatenate([mine, everything[:, width:]], axis=1)
-    routed = routed_sum(block, expert_gate_up[0], expert_down[0], cap)
     shared_units = shared_gate_up.shape[2]
     shared_pair = shared_gate_up.reshape(width, 2 * shared_units)
     both = jnp.dot(both_rows, shared_pair, preferred_element_type=jnp.float32)
     shared_hidden = (jax.nn.silu(both[:, :shared_units]) * both[:, shared_units:]).astype(
         jnp.bfloat16
     )
-    out_cols = jnp.dot(
-        lax.all_gather(shared_hidden, "dp", axis=1, tiled=True),
-        shared_down,
-        preferred_element_type=jnp.float32,
-    )
-    back = lax.all_to_all(routed + out_cols, "dp", split_axis=0, concat_axis=1, tiled=True)
-    total = resid.astype(jnp.float32) + back
+    routed, hidden = routed_sum(
+        block, expert_gate_up[0], expert_down[0], shared_hidden, cap
+    )
+    out_cols = jnp.dot(hidden[0], shared_down[:shared_units], preferred_element_type=jnp.float32)
+    out_cols += jnp.dot(hidden[1], shared_down[shared_units:], preferred_element_type=jnp.float32)
+    sums = (routed + out_cols).astype(jnp.bfloat16)
+    back = lax.all_to_all(sums, "dp", split_axis=0, concat_axis=1, tiled=True)
+    total = resid.astype(jnp.float32) + back.astype(jnp.float32)
     return rms_scale(total, final_gain).astype(jnp.bfloat16)
 
 

time: 126 us -> 119 us (0.944)
  blocking collectives: 27.7 us -> 20.1 us
    all_gather x1 -> x0, blocking collectives: 6.48 us -> none  [pair(): lax.all_gather(shared_hidden, 'dp', axis=1, tiled=True)]
  transfers between devices with their start and end apart: 1 -> 1, of which waited for: 0 -> 0; matrix products, arithmetic and copies ran while one was open for 10% -> 11% of each run, Pallas kernels for 0% -> 0%
where the time goes in v3:
time: 119 us; the launch traced here: 118 us
  Pallas kernels  67.7 us (57%)
  blocking collectives  20.1 us (17%)
  local copies, waits for them, and re-layouts  11.9 us (10%)
  matrix products  11.9 us (10%)
  starting transfers between devices  3.38 us (3%)
  other arithmetic  3.08 us (3%)
    pallas_call x1, Pallas kernels, routed_sum(): pl.pallas_call(functools.partial(routed_kernel, cap), out_shape=(jax.Shap...  67.7 us
    unnamed x17, local copies, waits for them, and re-layouts  11.4 us
    all_gather x1, blocking collectives, pair(): lax.all_gather(attention_out, 'dp', axis=0, tiled=True)  7.48 us
    all_to_all x1, blocking collectives, pair(): back = lax.all_to_all(sums, 'dp', split_axis=0, concat_axis=1, tiled=True)  6.85 us
    dot_general x1, matrix products, pair(): both = jnp.dot(both_rows, shared_pair, preferred_element_type=jnp.float32)  6.54 us
    all_gather x1, blocking collectives, pair(): lax.all_gather(jnp.concatenate([normed, aux], axis=1), 'dp', axis=0, tile...  5.73 us
    dot_general x1, matrix products, pair(): jnp.dot(lax.all_gather(attention_out, 'dp', axis=0, tiled=True), out_weig...  3.69 us
    all_to_all x1, starting transfers between devices, pair(): lax.all_to_all(proj_cols, 'dp', split_axis=0, concat_axis=1, tiled=True)  3.38 us
  transfers between devices with their start and end apart: 1, of which 0 were waited for; matrix products, arithmetic and copies ran while one was open for 11% of the time, Pallas kernels for 0%

profile of v3, /device:TPU:0, one launch (start us, length us, event | category | flops | bytes accessed | tf_op | source)
XLA Modules:
  0.0 118.3 jit_solution(2416021911066361807)
XLA Ops:
  0.0 7.5 %all_gather.6 = bf16[64,2048]{1,0:T(8,128)(2,1)S(1)} all-gather(bf16[32,2048]{1,0:T(8,128)(2,1)} %param.13), channel_id=1, replica_groups=mesh['dp'=2,'expert'=16] {'dp'}, dimensions={0}, use_global_device_ids=true | all-gather | bytes 393216 | tf_op jit(solution)/shard_map/all_gather | solution.py:410
  7.5 3.7 %convolution_convert_fusion = bf16[64,1024]{1,0:T(8,128)(2,1)} fusion(bf16[64,2048]{1,0:T(8,128)(2,1)S(1)} %all_gather.6, bf16[2048,1024]{1,0:T(8,128)(2,1)} %param.14), kind=kOutput, calls=%fused_computation.6 | convolution fusion | flops 268500992 | bytes 4587520 | tf_op jit(solution)/shard_map/dot_general | solution.py:409
  11.2 3.4 %all-to-all-start = ((bf16[2,32,1024]{2,1,0:T(8,128)(2,1)}), bf16[2,32,1024]{2,1,0:T(8,128)(2,1)S(1)}, u32[]{:S(2)}, u32[]{:S(2)}) async-start(bf16[2,32,1024]{2,1,0:T(8,128)(2,1)} %bitcast), calls=%async_computation | async-start | bytes 262144 | tf_op jit(solution)/shard_map/all_to_all | solution.py:414
  14.6 0.7 fusion.25
  15.3 0.7 iota_compare_fusion.3
  16.0 0.1 and_reduce_fusion
  16.1 0.1 copy.33
  16.2 0.1 fusion.14
  16.3 0.1 copy.36
  16.4 0.0 copy-start.5
  16.4 11.3 %copy.47 = bf16[256,8,2,1408]{3,1,2,0:T(8,128)(2,1)} copy(bf16[256,8,2,1408]{3,2,1,0:T(2,128)(2,1)} %bitcast.29) | data formatting | bytes 23068672
  27.8 0.2 fusion.16
  28.0 0.1 fusion.18
  28.1 0.3 fusion.26
  28.4 0.1 broadcast_divide_fusion
  28.4 0.1 copy.38
  28.5 0.1 select_reduce_fusion
  28.6 0.1 copy.40
  28.7 0.1 copy.39
  28.8 0.1 concatenate.9
  28.9 5.7 %all_gather.7 = bf16[64,2176]{1,0:T(8,128)(2,1)S(1)} all-gather(bf16[32,2176]{1,0:T(8,128)(2,1)S(1)} %concatenate.9), channel_id=1, replica_groups=mesh['dp'=2,'expert'=16] {'dp'}, dimensions={0}, use_global_device_ids=true | all-gather | bytes 417792 | tf_op jit(solution)/shard_map/all_gather | solution.py:433
  34.7 0.0 copy-start.1
  34.7 6.5 %fusion.19 = f32[64,2816]{1,0:T(8,128)S(1)} fusion(bf16[2048,2816]{1,0:T(8,128)(2,1)} %bitcast.28, bf16[64,2176]{1,0:T(8,128)(2,1)S(1)} %all_gather.7), kind=kOutput, calls=%fused_computation.20 | convolution fusion | flops 738197504 | bytes 12517376 | tf_op jit(solution)/shard_map/dot_general | solution.py:441
  41.2 0.0 slice-start
  41.2 0.1 fusion.15.hidden_ref
  41.4 0.0 slice-start.1
  41.4 67.7 %shard_map.118 = (f32[64,1024]{1,0:T(8,128)S(1)}, bf16[2,64,1408]{2,1,0:T(8,128)(2,1)S(1)}) custom-call(bf16[64,1152]{1,0:T(8,128)(2,1)S(1)} %pad_maximum_fusion.block_ref, bf16[1024,1408]{1,0:T(8,128)(2,1)S(1)} %bitcast.26, bf16[704,1024]{1,0:T(8,128)(2,1)S(1)} %bitcast.27, bf16[64,1408]{1,0:T(8,128)(2,1)S(1)} %fusion.15.hidden_ref), custom_call_target="tpu_custom_call" | custom-call | flops 5905580032 | bytes 4325376 | tf_op jit(solution)/shard_map/pallas_call | solution.py:347
  109.2 0.6 fusion
  109.8 0.6 fusion.10
  110.5 6.8 %all_to_all.26 = bf16[2,32,1024]{2,1,0:T(8,128)(2,1)S(1)} all-to-all(bf16[2,32,1024]{2,1,0:T(8,128)(2,1)S(1)} %bitcast.33), channel_id=1, replica_groups=mesh['dp'=2,'expert'=16] {'dp'}, dimensions={0} | all-to-all | bytes 262144 | tf_op jit(solution)/shard_map/all_to_all | solution.py:451
  117.4 0.2 multiply_reduce_fusion
  117.5 0.8 multiply_convert_fusion
  (26 shorter events, 0.2 us)
Async XLA Ops:
  0.0 28.1 %copy-start = (bf16[2048,16]{0,1:T(8,128)(2,1)S(1)}, bf16[2048,16]{0,1:T(8,128)(2,1)}, u32[]{:S(2)}) copy-start(bf16[2048,16]{0,1:T(8,128)(2,1)} %param.16) | copy-start | bytes 196612
  11.2 16.6 %all-to-all-start = ((bf16[2,32,1024]{2,1,0:T(8,128)(2,1)}), bf16[2,32,1024]{2,1,0:T(8,128)(2,1)S(1)}, u32[]{:S(2)}, u32[]{:S(2)}) async-start(bf16[2,32,1024]{2,1,0:T(8,128)(2,1)} %bitcast), calls=%async_computation | async-start | bytes 262144 | tf_op jit(solution)/shard_map/all_to_all | solution.py:414
  16.4 11.4 %copy-start.3 = (bf16[32,2048]{1,0:T(8,128)(2,1)S(1)}, bf16[32,2048]{1,0:T(8,128)(2,1)}, u32[]{:S(2)}) copy-start(bf16[32,2048]{1,0:T(8,128)(2,1)} %param.12) | copy-start | bytes 393220
  16.4 11.6 %copy-start.5 = (f32[2048]{0:T(1024)S(1)}, f32[2048]{0:T(1024)}, u32[]{:S(2)}) copy-start(f32[2048]{0:T(1024)} %param.15) | copy-start | bytes 24580
  34.7 6.7 %copy-start.1 = (bf16[1,1024,1408]{2,1,0:T(8,128)(2,1)S(1)}, bf16[1,1024,1408]{2,1,0:T(8,128)(2,1)}, u32[]{:S(2)}) copy-start(bf16[1,1024,1408]{2,1,0:T(8,128)(2,1)} %param.19) | copy-start | bytes 8650756
  34.7 6.7 %copy-start.2 = (bf16[1,704,1024]{2,1,0:T(8,128)(2,1)S(1)}, bf16[1,704,1024]{2,1,0:T(8,128)(2,1)}, u32[]{:S(2)}) copy-start(bf16[1,704,1024]{2,1,0:T(8,128)(2,1)} %param.20) | copy-start | bytes 4325380
  41.2 67.9 %slice-start = ((s8[5767168]{0:T(1024)(128)(4,1)}), s8[4194304]{0:T(1024)(128)(4,1)S(1)}, s32[]{:S(2)}) async-start(s8[5767168]{0:T(1024)(128)(4,1)} %bitcast.34), calls=%async_computation.2 | async-start | bytes 8388608
  41.4 67.8 %slice-start.1 = ((s8[5767168]{0:T(1024)(128)(4,1)}), s8[1572864]{0:T(1024)(128)(4,1)S(1)}, s32[]{:S(2)}) async-start(s8[5767168]{0:T(1024)(128)(4,1)} %bitcast.34), calls=%async_computation.3 | async-start | bytes 3145728
  109.2 8.4 %copy-start.4 = (f32[2048]{0:T(1024)S(1)}, f32[2048]{0:T(1024)}, u32[]{:S(2)}) copy-start(f32[2048]{0:T(1024)} %param.23) | copy-start | bytes 24580
